TPU v7x, 32 devices: a whole 2x2x4 slice. The times are simulated.
32 devices in a mesh: dom: 8 (over z, x), grp: 4 (over y, core).
Axes of the slice: x: 2, y: 2, z: 4, core: 2. Of those that a mesh axis runs over, the one named last changes fastest.
Arguments:
- node_latents: bfloat16 [4, 2048, 256], P('grp', 'dom'), may hold values from -6 to 6
- ghost_latents: bfloat16 [4, 512, 256], P('grp', 'dom'), may hold values from -6 to 6
- edge_latents: bfloat16 [4, 4096, 256], P('grp', 'dom'), may hold values from -6 to 6
- node_cotangent: bfloat16 [4, 2048, 256], P('grp', 'dom'), may hold values from -6 to 6
- edge_cotangent: bfloat16 [4, 4096, 256], P('grp', 'dom'), may hold values from -6 to 6
- senders: int32 [4, 4096], P('grp', 'dom'), may hold values from 0 to 319, as said below
- receivers: int32 [4, 4096], P('grp', 'dom'), may hold values from 0 to 255
- halo_counts: int32 [4, 32], P('grp', 'dom'), may hold values from 0 to 16, as said below
- recv_index: int32 [4, 32, 16], P('grp', 'dom'), may hold values from 0 to 255
- edge_w1: bfloat16 [768, 256], replicated, may hold values from -0.21875 to 0.21875
- edge_w2: bfloat16 [256, 256], replicated, may hold values from -0.375 to 0.375
- edge_w3: bfloat16 [256, 256], replicated, may hold values from -0.375 to 0.375
- edge_gain: float32 [256], replicated, may hold values from 0.5 to 1.5
- node_w1: bfloat16 [512, 256], replicated, may hold values from -0.25 to 0.25
- node_w2: bfloat16 [256, 256], replicated, may hold values from -0.375 to 0.375
- node_w3: bfloat16 [256, 256], replicated, may hold values from -0.375 to 0.375
- node_gain: float32 [256], replicated, may hold values from 0.5 to 1.5
Outputs:
- grad_node: bfloat16 [4, 2048, 256], P('grp', 'dom')
- grad_edge: bfloat16 [4, 4096, 256], P('grp', 'dom')
- grad_edge_w1: float32 [768, 256], P('grp')
- grad_edge_w2: float32 [256, 256], P('grp')
- grad_edge_w3: float32 [256, 256], P('grp')
- grad_edge_gain: float32 [256], P('grp')
- grad_node_w1: float32 [512, 256], P('grp')
- grad_node_w2: float32 [256, 256], P('grp')
- grad_node_w3: float32 [256, 256], P('grp')
- grad_node_gain: float32 [256], P('grp')
Inputs may be any that keep to these rules, and one draw needn't show every extreme that they name: Ghost senders name only live slots, s below halo_counts of their direction; every other sender is an owned node. `halo_counts`: directions that point past the group's ends hold 0; every partition has a direction holding exactly 16.
All inputs are finite; a program needn't handle non-finite values.
Results may differ from a plain program's by a relative error of at most 0.013.
Values may be sent and summed in bfloat16 or wider, within the bound.
A program may use at most 64 MiB of HBM per device.

v0:
```python
import math

import jax
import jax.numpy as jnp
from jax import lax
from jax.sharding import PartitionSpec as P

EPS = 1e-05
OFFSETS = (-2, -1, 1, 2)


def from_behind(block, axis, distance):
    devices = range(lax.axis_size(axis))
    route = [(i - distance, i) for i in devices if i - distance in devices]
    return lax.ppermute(block, axis, route)


def matmul(left, right):
    return jnp.dot(left, right, preferred_element_type=jnp.float32)


def over_rows(left, right):
    return lax.dot_general(
        left, right, (((0,), (0,)), ((), ())), preferred_element_type=jnp.float32
    )


def against(left, weight):
    return lax.dot_general(
        left, weight, (((1,), (1,)), ((), ())), preferred_element_type=jnp.float32
    )


def silu_slope(value):
    sigma = jax.nn.sigmoid(value)
    return sigma * (1.0 + value * (1.0 - sigma))


def norm_parts(value):
    centre = value - jnp.mean(value, axis=-1, keepdims=True)
    scale = lax.rsqrt(jnp.mean(centre * centre, axis=-1, keepdims=True) + EPS)
    return (centre * scale, scale)


def norm_back(upstream, normed, scale):
    return scale * (
        upstream
        - jnp.mean(upstream, axis=-1, keepdims=True)
        - normed * jnp.mean(upstream * normed, axis=-1, keepdims=True)
    )


def mlp_forward(inputs, first_w, second_w, third_w, gain):
    pre_one = matmul(inputs, first_w)
    act_one = jax.nn.silu(pre_one).astype(jnp.bfloat16)
    pre_two = matmul(act_one, second_w)
    act_two = jax.nn.silu(pre_two).astype(jnp.bfloat16)
    normed, scale = norm_parts(matmul(act_two, third_w))
    return (normed * gain, (pre_one, act_one, pre_two, act_two, normed, scale))


def mlp_backward(inputs, first_w, second_w, third_w, gain, saved, upstream):
    pre_one, act_one, pre_two, act_two, normed, scale = saved
    grad_gain = jnp.sum(upstream * normed, axis=0)
    delta_out = norm_back(upstream * gain, normed, scale).astype(jnp.bfloat16)
    grad_third = over_rows(act_two, delta_out)
    delta_two = (against(delta_out, third_w) * silu_slope(pre_two)).astype(jnp.bfloat16)
    grad_second = over_rows(act_one, delta_two)
    delta_one = (against(delta_two, second_w) * silu_slope(pre_one)).astype(jnp.bfloat16)
    grad_first = over_rows(inputs, delta_one)
    return (against(delta_one, first_w), (grad_first, grad_second, grad_third, grad_gain))


def local_pass(
    node_lat, ghost_lat, edge_lat, node_cot, edge_cot, sender_ids, receiver_ids, counts, weights
):
    edge_one, edge_two, edge_three, edge_g, node_one, node_two, node_three, node_g = weights
    node_count = node_lat.shape[0]
    ghost_count = ghost_lat.shape[0]
    slot_count = ghost_count // 4
    latent = node_lat.shape[1]
    node_table = jnp.concatenate([node_lat, ghost_lat], axis=0)
    send_hot = (
        sender_ids[:, None] == lax.iota(jnp.int32, node_count + ghost_count)[None, :]
    ).astype(jnp.bfloat16)
    recv_hot = (receiver_ids[:, None] == lax.iota(jnp.int32, node_count)[None, :]).astype(
        jnp.bfloat16
    )
    sender_lat = matmul(send_hot, node_table).astype(jnp.bfloat16)
    receiver_lat = matmul(recv_hot, node_lat).astype(jnp.bfloat16)
    edge_in = jnp.concatenate([edge_lat, sender_lat, receiver_lat], axis=1)
    message, edge_saved = mlp_forward(edge_in, edge_one, edge_two, edge_three, edge_g)
    updated = (edge_lat.astype(jnp.float32) + message).astype(jnp.bfloat16)
    summed = over_rows(recv_hot, updated).astype(jnp.bfloat16)
    node_in = jnp.concatenate([node_lat, summed], axis=1)
    unused_out, node_saved = mlp_forward(node_in, node_one, node_two, node_three, node_g)
    node_up = node_cot.astype(jnp.float32)
    node_grad_in, node_terms = mlp_backward(
        node_in, node_one, node_two, node_three, node_g, node_saved, node_up
    )
    back_summed = node_grad_in[:, latent:].astype(jnp.bfloat16)
    edge_up = edge_cot.astype(jnp.float32) + matmul(recv_hot, back_summed)
    edge_grad_in, edge_terms = mlp_backward(
        edge_in, edge_one, edge_two, edge_three, edge_g, edge_saved, edge_up
    )
    grad_edge = (edge_up + edge_grad_in[:, :latent]).astype(jnp.bfloat16)
    to_sender = edge_grad_in[:, latent : 2 * latent].astype(jnp.bfloat16)
    to_receiver = edge_grad_in[:, 2 * latent :].astype(jnp.bfloat16)
    to_table = over_rows(send_hot, to_sender)
    node_total = (
        node_up
        + node_grad_in[:, :latent]
        + over_rows(recv_hot, to_receiver)
        + to_table[:node_count]
    )
    ghost_grad = to_table[node_count:].reshape(4, slot_count, latent)
    is_live = lax.iota(jnp.int32, slot_count)[None, :] < counts[:, None]
    ghost_grad = jnp.where(is_live[:, :, None], ghost_grad, 0.0).astype(jnp.bfloat16)
    return (grad_edge, node_total, ghost_grad, edge_terms + node_terms)


def per_device(
    node_latents,
    ghost_latents,
    edge_latents,
    node_cotangent,
    edge_cotangent,
    senders,
    receivers,
    halo_counts,
    recv_index,
    edge_w1,
    edge_w2,
    edge_w3,
    edge_gain,
    node_w1,
    node_w2,
    node_w3,
    node_gain,
):
    weights = (edge_w1, edge_w2, edge_w3, edge_gain, node_w1, node_w2, node_w3, node_gain)
    grad_edge, node_total, ghost_grad, grad_terms = local_pass(
        node_latents[0],
        ghost_latents[0],
        edge_latents[0],
        node_cotangent[0],
        edge_cotangent[0],
        senders[0],
        receivers[0],
        halo_counts[0],
        weights,
    )
    (
        edge_first,
        edge_second,
        edge_third,
        edge_gsum,
        node_first,
        node_second,
        node_third,
        node_gsum,
    ) = grad_terms
    domains = lax.axis_size("dom")
    groups = lax.axis_size("grp")
    reduced = (
        lax.psum_scatter(
            edge_first.astype(jnp.bfloat16), "grp", scatter_dimension=0, tiled=True
        ).astype(jnp.float32),
        lax.psum_scatter(
            edge_second.astype(jnp.bfloat16), "grp", scatter_dimension=0, tiled=True
        ).astype(jnp.float32),
        lax.psum_scatter(
            edge_third.astype(jnp.bfloat16), "grp", scatter_dimension=0, tiled=True
        ).astype(jnp.float32),
        lax.psum_scatter(
            edge_gsum.astype(jnp.bfloat16), "grp", scatter_dimension=0, tiled=True
        ).astype(jnp.float32),
        lax.psum_scatter(
            node_first.astype(jnp.bfloat16), "grp", scatter_dimension=0, tiled=True
        ).astype(jnp.float32),
        lax.psum_scatter(
            node_second.astype(jnp.bfloat16), "grp", scatter_dimension=0, tiled=True
        ).astype(jnp.float32),
        lax.psum_scatter(
            node_third.astype(jnp.bfloat16), "grp", scatter_dimension=0, tiled=True
        ).astype(jnp.float32),
        lax.psum_scatter(
            node_gsum.astype(jnp.bfloat16), "grp", scatter_dimension=0, tiled=True
        ).astype(jnp.float32),
    )
    reduced = lax.psum(
        (
            reduced[0],
            reduced[1],
            reduced[2],
            reduced[3],
            reduced[4],
            reduced[5],
            reduced[6],
            reduced[7],
        ),
        "dom",
    )
    arrivals = []
    for direction, offset in enumerate(OFFSETS):
        arrivals.append(from_behind(ghost_grad[direction], "dom", offset))
    arrived = jnp.stack(arrivals)
    node_count = node_total.shape[0]
    targets = recv_index[0].reshape(-1)
    owner_hot = (lax.iota(jnp.int32, node_count)[:, None] == targets[None, :]).astype(jnp.bfloat16)
    node_total = node_total + matmul(owner_hot, arrived.reshape(targets.shape[0], -1))
    grad_node = node_total.astype(jnp.bfloat16)[None]
    partitions = domains * groups
    edge_scale = 1.0 / math.sqrt(partitions * edge_latents.shape[1])
    node_scale = 1.0 / math.sqrt(partitions * node_latents.shape[1])
    return (
        grad_node,
        grad_edge[None],
        reduced[0] * edge_scale,
        reduced[1] * edge_scale,
        reduced[2] * edge_scale,
        reduced[3] * edge_scale,
        reduced[4] * node_scale,
        reduced[5] * node_scale,
        reduced[6] * node_scale,
        reduced[7] * node_scale,
    )


def solution(mesh):
    placed = (
        P("grp", "dom", None),
        P("grp", "dom", None),
        P("grp", "dom", None),
        P("grp", "dom", None),
        P("grp", "dom", None),
        P("grp", "dom"),
        P("grp", "dom"),
        P("grp", "dom"),
        P("grp", "dom", None),
        P(),
        P(),
        P(),
        P(),
        P(),
        P(),
        P(),
        P(),
    )
    return jax.shard_map(
        per_device,
        mesh=mesh,
        in_specs=placed,
        out_specs=(
            P("grp", "dom", None),
            P("grp", "dom", None),
            P("grp", None),
            P("grp", None),
            P("grp", None),
            P("grp"),
            P("grp", None),
            P("grp", None),
            P("grp", None),
            P("grp"),
        ),
        check_vma=False,
    )
```

profile of v0, /device:TPU:0, one launch (start us, length us, event | category | flops | bytes accessed | tf_op | source)
XLA Modules:
  0.0 210.2 jit_solution(12749347107863953424)
XLA Ops:
  7.2 0.9 copy.42
  8.2 1.0 copy.39
  9.2 1.1 copy.40
  10.2 1.1 copy.41
  11.4 1.3 convolution_convert_fusion.2
  12.7 1.1 convolution_convert_fusion.3
  13.8 1.2 multiply_convert_fusion.2
  15.1 1.0 multiply_convert_fusion.1
  16.1 0.3 fusion.43
  16.5 0.4 convolution_convert_fusion.6
  16.9 0.1 copy-done.6
  17.1 0.3 fusion.32
  17.3 0.2 fusion.41
  17.6 0.3 fusion.44
  18.0 0.7 fusion.18
  18.8 0.9 convolution_convert_fusion.7
  19.9 0.2 fusion.3
  20.1 0.9 convolution_convert_fusion.8
  21.1 0.2 fusion.4
  21.4 0.1 copy.44
  21.5 0.5 copy-done.12
  22.0 0.3 fusion.46
  22.3 1.0 multiply_reduce_fusion
  23.4 0.2 multiply_convert_fusion
  23.5 0.3 fusion
  23.9 0.6 copy-done.9
  24.5 0.9 convolution_convert_fusion.5
  25.5 0.9 convolution_convert_fusion.4
  26.5 1.8 convolution_convert_fusion.1
  28.5 1.4 fusion.1
  29.9 0.4 fusion.45
  30.3 0.2 copy-done.25
  30.6 0.5 fusion.7
  31.0 0.7 copy-done.5
  31.8 0.6 slice_bitcast_fusion.3
  32.5 1.3 collective-permute-start
  33.7 6.2 %collective-permute-start.3 = (bf16[16,256]{1,0:T(8,128)(2,1)}, bf16[16,256]{1,0:T(8,128)(2,1)}, u32[]{:S(2)}, u32[]{:S(2)}) collective-permute-start(bf16[16,256]{1,0:T(8,128)(2,1)} %get-tuple-element.47), channel_id=1, source_target_pairs={{0,8},{4,12},{8,16},{12,20},{16,24},{20,28},{1,9},{5,13},{9,17},{1... | collective-permute-start | bytes 24584 | tf_op jit(solution)/shard_map/ppermute | solution.py:15
  39.9 4.4 %collective-permute-start.2 = (bf16[16,256]{1,0:T(8,128)(2,1)}, bf16[16,256]{1,0:T(8,128)(2,1)}, u32[]{:S(2)}, u32[]{:S(2)}) collective-permute-start(bf16[16,256]{1,0:T(8,128)(2,1)} %get-tuple-element.48), channel_id=1, source_target_pairs={{0,4},{4,8},{8,12},{12,16},{16,20},{20,24},{24,28},{1,5},{5,9},{9,... | collective-permute-start | bytes 24584 | tf_op jit(solution)/shard_map/ppermute | solution.py:15
  44.3 1.3 collective-permute-start.1
  45.6 1.1 convolution_convert_fusion
  46.8 1.0 slice.51
  47.8 0.1 copy.53
  48.1 2.0 fusion.2
  50.2 0.2 copy.55
  50.4 1.2 dynamic-slice
  52.3 5.9 %all-reduce.3 = (bf16[256]{0:T(256)(128)(2,1)S(1)}, bf16[256]{0:T(256)(128)(2,1)S(1)}) all-reduce(bf16[256]{0:T(256)(128)(2,1)S(1)} %copy-done.20, bf16[256]{0:T(256)(128)(2,1)} %get-tuple-element.33), channel_id=5, replica_groups=mesh['dom'=8,'grp'=4] {'grp'}, use_global_device_ids=true, to_apply=%region_15.16.clone | all-reduce | flops 512 | bytes 2048
  58.5 0.8 copy.50
  59.4 0.8 pad_maximum_fusion.6
  60.2 0.2 fusion.6
  60.4 0.8 copy.49
  61.2 3.3 %reduce-scatter.15.cloned.1.call-done = bf16[64,256]{1,0:T(8,128)(2,1)} async-done(((bf16[256,256]{1,0:T(8,128)(2,1)}), bf16[64,256]{1,0:T(8,128)(2,1)}) %reduce-scatter.15.cloned.1.call-update) | async-done | bytes 32784 | tf_op jit(solution)/shard_map/reduce_scatter | solution.py:181
  64.4 22.7 %reduce-scatter.9.cloned.1.call-done = bf16[64,256]{1,0:T(8,128)(2,1)} async-done(((bf16[256,256]{1,0:T(8,128)(2,1)}), bf16[64,256]{1,0:T(8,128)(2,1)}) %reduce-scatter.9.cloned.1.call-update) | async-done | bytes 32784 | tf_op jit(solution)/shard_map/reduce_scatter | solution.py:169
  87.1 22.0 %reduce-scatter.11.cloned.1.call-done = bf16[64,256]{1,0:T(8,128)(2,1)} async-done(((bf16[256,256]{1,0:T(8,128)(2,1)}), bf16[64,256]{1,0:T(8,128)(2,1)}) %reduce-scatter.11.cloned.1.call-update) | async-done | bytes 32784 | tf_op jit(solution)/shard_map/reduce_scatter | solution.py:172
  109.1 22.4 %reduce-scatter.13.cloned.1.call-done = bf16[128,256]{1,0:T(8,128)(2,1)} async-done(((bf16[512,256]{1,0:T(8,128)(2,1)}), bf16[128,256]{1,0:T(8,128)(2,1)}) %reduce-scatter.13.cloned.1.call-update) | async-done | bytes 65552 | tf_op jit(solution)/shard_map/reduce_scatter | solution.py:178
  131.5 23.4 %reduce-scatter.7.cloned.1.call-done = bf16[192,256]{1,0:T(8,128)(2,1)} async-done(((bf16[768,256]{1,0:T(8,128)(2,1)}), bf16[192,256]{1,0:T(8,128)(2,1)}) %reduce-scatter.7.cloned.1.call-update) | async-done | bytes 98320 | tf_op jit(solution)/shard_map/reduce_scatter | solution.py:166
  154.8 43.6 %all-reduce.5 = (f32[192,256]{1,0:T(8,128)S(1)}, f32[64,256]{1,0:T(8,128)S(1)}, f32[64,256]{1,0:T(8,128)S(1)}, f32[64]{0:T(128)S(1)}, f32[128,256]{1,0:T(8,128)S...) all-reduce(bf16[192,256]{1,0:T(8,128)(2,1)} %reduce-scatter.7.clone, ...), channel_id=1, replica_groups=mesh['dom'=8,'grp'=4] {'dom'}, use_global_device_ids=true, to_apply=%region_9.10 | all-reduce | flops 147584 | bytes 885760 | tf_op jit(solution)/shard_map/psum | solution.py:191
  198.5 0.7 broadcast_multiply_fusion
  199.2 0.5 broadcast_multiply_fusion.13
  199.7 0.5 broadcast_multiply_fusion.12
  200.2 0.6 broadcast_multiply_fusion.5
  200.8 0.6 broadcast_multiply_fusion.4
  201.4 0.6 broadcast_multiply_fusion.3
  202.1 0.6 broadcast_multiply_fusion.2
  202.7 0.7 broadcast_multiply_fusion.1
  (94 shorter events, 1.6 us)
Async XLA Ops:
  7.2 6.6 %copy-start = (bf16[768,256]{1,0:T(8,128)(2,1)S(1)}, bf16[768,256]{1,0:T(8,128)(2,1)}, u32[]{:S(2)}) copy-start(bf16[768,256]{1,0:T(8,128)(2,1)} %param.26) | copy-start | bytes 1179652
  7.2 54.0 %reduce-scatter.17.cloned.1.call-start = ((), (), s32[]{:S(2)}) async-start(), calls=%async_computation.11 | async-start | bytes 163840 | tf_op jit(solution)/shard_map/reduce_scatter | solution.py:184
  9.2 9.6 %copy-start.1 = (bf16[1,256,256]{1,2,0:T(8,128)(2,1)}, bf16[1,256,256]{1,2,0:T(8,128)(2,1)S(1)}, u32[]{:S(2)}) copy-start(bf16[1,256,256]{1,2,0:T(8,128)(2,1)S(1)} %copy.39) | copy-start | bytes 393220
  10.2 6.7 %copy-start.14 = (bf16[1,256,256]{1,2,0:T(8,128)(2,1)}, bf16[1,256,256]{1,2,0:T(8,128)(2,1)S(1)}, u32[]{:S(2)}) copy-start(bf16[1,256,256]{1,2,0:T(8,128)(2,1)S(1)} %copy.40) | copy-start | bytes 393220
  13.8 1.2 copy-start.28
  13.8 1.2 copy-start.23
  15.1 1.3 copy-start.8
  15.1 1.1 copy-start.10
  15.1 1.5 copy-start.16
  15.1 1.5 copy-start.18
  16.1 0.9 copy-start.6
  16.1 1.2 copy-start.22
  16.5 1.1 copy-start.21
  17.0 0.8 copy-start.27
  17.3 0.7 copy-start.17
  19.8 44.6 %reduce-scatter.15.cloned.1.call-start = ((), (), s32[]{:S(2)}) async-start(), calls=%async_computation.10 | async-start | bytes 163840 | tf_op jit(solution)/shard_map/reduce_scatter | solution.py:181
  20.1 1.3 copy-start.7
  21.1 66.0 %reduce-scatter.9.cloned.1.call-start = ((), (), s32[]{:S(2)}) async-start(), calls=%async_computation.7 | async-start | bytes 163840 | tf_op jit(solution)/shard_map/reduce_scatter | solution.py:169
  21.4 0.7 copy-start.12
  22.3 1.2 copy-start.11
  22.3 1.2 copy-start.30
  23.5 1.0 copy-start.9
  24.5 2.0 copy-start.13
  24.5 2.0 copy-start.15
  24.5 3.9 %copy-start.26 = (s32[1,4]{1,0:T(1,128)S(1)}, s32[1,4]{1,0:T(1,128)}, u32[]{:S(2)}) copy-start(s32[1,4]{1,0:T(1,128)} %param.24) | copy-start | bytes 52
  24.5 4.0 %copy-start.24 = (bf16[256,256]{1,0:T(8,128)(2,1)S(1)}, bf16[256,256]{1,0:T(8,128)(2,1)}, u32[]{:S(2)}) copy-start(bf16[256,256]{1,0:T(8,128)(2,1)} %param.27) | copy-start | bytes 393220
  25.4 83.7 %reduce-scatter.11.cloned.1.call-start = ((), (), s32[]{:S(2)}) async-start(), calls=%async_computation.8 | async-start | bytes 163840 | tf_op jit(solution)/shard_map/reduce_scatter | solution.py:172
  26.4 105.0 %reduce-scatter.13.cloned.1.call-start = ((), (), s32[]{:S(2)}) async-start(), calls=%async_computation.9 | async-start | bytes 327680 | tf_op jit(solution)/shard_map/reduce_scatter | solution.py:178
  28.4 126.5 %reduce-scatter.7.cloned.1.call-start = ((), (), s32[]{:S(2)}) async-start(), calls=%async_computation.6 | async-start | bytes 491520 | tf_op jit(solution)/shard_map/reduce_scatter | solution.py:166
  29.9 0.7 copy-start.25
  29.9 15.7 %copy-start.29 = (bf16[512,256]{0,1:T(8,128)(2,1)S(1)}, bf16[512,256]{0,1:T(8,128)(2,1)}, u32[]{:S(2)}) copy-start(bf16[512,256]{0,1:T(8,128)(2,1)} %copy-done.28) | copy-start | bytes 786436
  30.3 15.3 %copy-start.3 = (bf16[512,768]{1,0:T(8,128)(2,1)}, bf16[512,768]{1,0:T(8,128)(2,1)S(1)}, u32[]{:S(2)}) copy-start(bf16[512,768]{1,0:T(8,128)(2,1)S(1)} %get-tuple-element.59) | copy-start | bytes 2359300
  31.0 0.7 copy-start.5
  32.5 26.9 %collective-permute-start = (bf16[16,256]{1,0:T(8,128)(2,1)}, bf16[16,256]{1,0:T(8,128)(2,1)}, u32[]{:S(2)}, u32[]{:S(2)}) collective-permute-start(bf16[16,256]{1,0:T(8,128)(2,1)} %get-tuple-element.46), channel_id=1, source_target_pairs={{8,0},{12,4},{16,8},{20,12},{24,16},{28,20},{9,1},{13,5},{17,9},{2... | collective-permute-start | bytes 24584 | tf_op jit(solution)/shard_map/ppermute | solution.py:15
  33.7 25.6 %collective-permute-start.3 = (bf16[16,256]{1,0:T(8,128)(2,1)}, bf16[16,256]{1,0:T(8,128)(2,1)}, u32[]{:S(2)}, u32[]{:S(2)}) collective-permute-start(bf16[16,256]{1,0:T(8,128)(2,1)} %get-tuple-element.47), channel_id=1, source_target_pairs={{0,8},{4,12},{8,16},{12,20},{16,24},{20,28},{1,9},{5,13},{9,17},{1... | collective-permute-start | bytes 24584 | tf_op jit(solution)/shard_map/ppermute | solution.py:15
  39.9 19.5 %collective-permute-start.2 = (bf16[16,256]{1,0:T(8,128)(2,1)}, bf16[16,256]{1,0:T(8,128)(2,1)}, u32[]{:S(2)}, u32[]{:S(2)}) collective-permute-start(bf16[16,256]{1,0:T(8,128)(2,1)} %get-tuple-element.48), channel_id=1, source_target_pairs={{0,4},{4,8},{8,12},{12,16},{16,20},{20,24},{24,28},{1,5},{5,9},{9,... | collective-permute-start | bytes 24584 | tf_op jit(solution)/shard_map/ppermute | solution.py:15
  44.3 15.1 %collective-permute-start.1 = (bf16[16,256]{1,0:T(8,128)(2,1)S(1)}, bf16[16,256]{1,0:T(8,128)(2,1)}, u32[]{:S(2)}, u32[]{:S(2)}) collective-permute-start(bf16[16,256]{1,0:T(8,128)(2,1)S(1)} %get-tuple-element.49), channel_id=1, source_target_pairs={{4,0},{8,4},{12,8},{16,12},{20,16},{24,20},{28,24},{5,1},{9,5},{13... | collective-permute-start | bytes 24584 | tf_op jit(solution)/shard_map/ppermute | solution.py:15
  46.7 1.3 copy-start.2
  50.1 2.2 %copy-start.20 = (bf16[256]{0:T(256)(128)(2,1)S(1)}, bf16[256]{0:T(256)(128)(2,1)}, u32[]{:S(2)}) copy-start(bf16[256]{0:T(256)(128)(2,1)} %get-tuple-element.30) | copy-start | bytes 1540
  50.1 8.3 %copy-start.19 = (s32[1,4,16]{2,1,0:T(4,128)S(1)}, s32[1,4,16]{2,1,0:T(4,128)}, u32[]{:S(2)}) copy-start(s32[1,4,16]{2,1,0:T(4,128)} %param.25) | copy-start | bytes 772
  50.2 10.0 %copy-start.4 = (f32[256,256]{0,1:T(8,128)S(1)}, f32[256,256]{0,1:T(8,128)}, u32[]{:S(2)}) copy-start(f32[256,256]{0,1:T(8,128)} %fusion.2) | copy-start | bytes 786436
Sparse Core Ops, SparseCore 0:
  19.9 22.2 reduce-scatter.16
  44.8 19.5 reduce-scatter.14
  67.4 19.6 reduce-scatter.8
  89.5 19.5 reduce-scatter.10
  111.4 20.0 reduce-scatter.12
  134.0 20.8 reduce-scatter.6
where the time goes:
time: 211 us; the launch traced here: 210 us
  waiting for transfers between devices  93.8 us (44%)
  blocking collectives  49.5 us (23%)
  matrix products  19.3 us (9%)
  between operations  15.3 us (7%)
  starting transfers between devices  13.4 us (6%)
  local copies, waits for them, and re-layouts  11.7 us (6%)
  other arithmetic  7.22 us (3%)
    psum x1, blocking collectives, per_device(): lax.psum((reduced[0], reduced[1], reduced[2], reduced[3], reduced[4], red...  43.6 us
    reduce_scatter x1, waiting for transfers between devices, per_device(): lax.psum_scatter(edge_first.astype(jnp.bfloat16), 'grp', scatter_dimensio...  23.4 us
    reduce_scatter x1, waiting for transfers between devices, per_device(): lax.psum_scatter(edge_second.astype(jnp.bfloat16), 'grp', scatter_dimensi...  22.7 us
    reduce_scatter x1, waiting for transfers between devices, per_device(): lax.psum_scatter(node_first.astype(jnp.bfloat16), 'grp', scatter_dimensio...  22.4 us
    reduce_scatter x1, waiting for transfers between devices, per_device(): lax.psum_scatter(edge_third.astype(jnp.bfloat16), 'grp', scatter_dimensio...  22 us
    ppermute x4, starting transfers between devices, from_behind(): return lax.ppermute(block, axis, route)  13.1 us
    unnamed x73, local copies, waits for them, and re-layouts  9.99 us
    dot_general x9, matrix products, over_rows(): lax.dot_general(left, right, (((0,), (0,)), ((), ())), preferred_element_...  9.55 us
  transfers between devices with their start and end apart: 10, of which 5 were waited for; matrix products, arithmetic and copies ran while one was open for 9% of the time, Pallas kernels for 0%

commit v1 on v0

--- a/solution.py
+++ b/solution.py
@@ -1,8 +1,11 @@
+import functools
 import math
 
 import jax
 import jax.numpy as jnp
 from jax import lax
+from jax.experimental import pallas as pl
+from jax.experimental.pallas import tpu as pltpu
 from jax.sharding import PartitionSpec as P
 
 EPS = 1e-05
@@ -227,6 +230,458 @@
     )
 
 
+MESH = pl.DeviceIdType.MESH
+
+
+def one_hot(mask):
+    return jnp.where(mask, 1.0, 0.0).astype(jnp.bfloat16)
+
+
+def hot_pair(ids, count):
+    edges = ids.shape[1]
+    column = jnp.transpose(jnp.broadcast_to(ids, (128, edges)))
+    blocks = []
+    for start in range(0, count, 128):
+        width = min(128, count - start)
+        lane = lax.broadcasted_iota(jnp.int32, (edges, width), 1) + start
+        blocks.append(one_hot(column[:, :width] == lane))
+    row = lax.broadcasted_iota(jnp.int32, (count, edges), 0)
+    return blocks, one_hot(ids == row)
+
+
+def wide(value):
+    return value.astype(jnp.float32)
+
+
+def narrow(value):
+    return value.astype(jnp.bfloat16)
+
+
+def activate(pre):
+    sigma = jax.nn.sigmoid(pre)
+    return narrow(pre * sigma), sigma * (1.0 + pre * (1.0 - sigma))
+
+
+def fused_kernel(
+    plan,
+    node_lat,
+    ghost_lat,
+    edge_lat,
+    node_cot,
+    edge_cot,
+    senders,
+    receivers,
+    counts,
+    recv_index,
+    ew1,
+    ew2,
+    ew3,
+    egain,
+    nw1,
+    nw2,
+    nw3,
+    ngain,
+    grad_node,
+    grad_edge,
+    out_e1,
+    out_e2,
+    out_e3,
+    out_eg,
+    out_n1,
+    out_n2,
+    out_n3,
+    out_ng,
+    terms_n,
+    terms_b,
+    terms_c,
+    core_n,
+    core_b,
+    core_c,
+    half_n,
+    half_b,
+    half_c,
+    keep_n,
+    keep_b,
+    keep_c,
+    side_n,
+    side_b,
+    side_c,
+    part_n,
+    part_b,
+    part_c,
+    gath_n,
+    gath_b,
+    gath_c,
+    fin_n,
+    fin_b,
+    fin_c,
+    ghost_out,
+    ghost_in,
+    send_sem,
+    recv_sem,
+):
+    domains, edge_scale, node_scale = plan
+    latent = node_lat.shape[1]
+    owned = node_lat.shape[0]
+    ghosts = ghost_lat.shape[0]
+    slots = ghosts // 4
+    blocks = domains // 2
+    half = latent // 2
+    dom = lax.axis_index("dom")
+    grp = lax.axis_index("grp")
+    core = lax.rem(grp, 2)
+    pair = lax.div(grp, 2)
+    other_core = 2 * pair + 1 - core
+    other_pair = 2 * (1 - pair) + core
+    per_chunk = 2 + 2 * (domains - 1)
+
+    def ahead(step):
+        return lax.rem(dom + step + domains, domains)
+
+    barrier = pltpu.get_barrier_semaphore()
+    pl.semaphore_signal(barrier, inc=1, device_id={"grp": other_core}, device_id_type=MESH)
+    pl.semaphore_signal(barrier, inc=1, device_id={"grp": other_pair}, device_id_type=MESH)
+    for step in range(1, domains):
+        pl.semaphore_signal(barrier, inc=1, device_id={"dom": ahead(step)}, device_id_type=MESH)
+
+    def remote(src, dst, number, target):
+        return pltpu.make_async_remote_copy(
+            src_ref=src,
+            dst_ref=dst,
+            send_sem=send_sem.at[number],
+            recv_sem=recv_sem.at[number],
+            device_id=target,
+            device_id_type=MESH,
+        )
+
+    chunks = (
+        (terms_n, core_n, half_n, keep_n, side_n, part_n, gath_n, fin_n),
+        (terms_b, core_b, half_b, keep_b, side_b, part_b, gath_b, fin_b),
+        (terms_c, core_c, half_c, keep_c, side_c, part_c, gath_c, fin_c),
+    )
+
+    def put(number, matrices, tail=None):
+        terms = chunks[number][0]
+        for quarter in range(4):
+            rows = []
+            for matrix in matrices:
+                share = matrix.shape[0] // 4
+                rows.append(matrix[quarter * share : (quarter + 1) * share])
+            rows = narrow(rows[0] if len(rows) == 1 else jnp.concatenate(rows, axis=0))
+            size = rows.shape[0] // blocks
+            for piece in range(domains):
+                at = (piece // 2) * size
+                lane = (piece % 2) * half
+                terms[quarter % 2, quarter // 2, piece, 0:size] = rows[
+                    at : at + size, lane : lane + half
+                ]
+                if tail is not None:
+                    terms[quarter % 2, quarter // 2, piece, size : size + 16] = tail
+
+    def over_core(number):
+        terms, arrived = chunks[number][0:2]
+        return remote(
+            terms.at[1 - core], arrived, number * per_chunk, {"grp": other_core}
+        )
+
+    def over_pair(number):
+        return remote(
+            chunks[number][2], chunks[number][4], number * per_chunk + 1, {"grp": other_pair}
+        )
+
+    def over_dom(number):
+        part, gath = chunks[number][5:7]
+        return [
+            remote(
+                part.at[ahead(step)],
+                gath.at[step],
+                number * per_chunk + 1 + step,
+                {"dom": ahead(step)},
+            )
+            for step in range(1, domains)
+        ]
+
+    def spread(number):
+        fin = chunks[number][7]
+        return [
+            remote(
+                fin.at[0],
+                fin.at[step],
+                number * per_chunk + domains + step,
+                {"dom": ahead(step)},
+            )
+            for step in range(1, domains)
+        ]
+
+    def stage_pair(number):
+        terms, arrived, send, keep = chunks[number][0:4]
+        over_core(number).wait()
+        send[...] = narrow(wide(terms[core, 1 - pair]) + wide(arrived[1 - pair]))
+        over_pair(number).start()
+        keep[...] = wide(terms[core, pair]) + wide(arrived[pair])
+
+    def stage_dom(number):
+        keep, side, part = chunks[number][3:6]
+        over_pair(number).wait()
+        part[...] = narrow(keep[...] + wide(side[...]))
+        for copy in over_dom(number):
+            copy.start()
+
+    def stage_spread(number):
+        part, gath, fin = chunks[number][5:8]
+        for copy in over_dom(number):
+            copy.wait()
+        total = wide(part[dom])
+        for step in range(1, domains):
+            total = total + wide(gath[step])
+        fin[0] = narrow(total[: fin.shape[1]])
+        for copy in spread(number):
+            copy.start()
+        return total
+
+    def stage_out(number, outs, scale):
+        fin = chunks[number][7]
+        for copy in spread(number):
+            copy.wait()
+        size = fin.shape[1]
+        for piece in range(domains):
+            value = wide(fin[lax.rem(dom - piece + domains, domains)]) * scale
+            lane = (piece % 2) * half
+            first = (piece // 2) * size
+            base = 0
+            for out in outs:
+                low, high = max(first, base), min(first + size, base + out.shape[0])
+                if low < high:
+                    out[low - base : high - base, lane : lane + half] = value[
+                        low - first : high - first
+                    ]
+                base += out.shape[0]
+
+    sender_blocks, sender_rows = hot_pair(senders[...], owned + ghosts)
+    receiver_blocks, receiver_rows = hot_pair(receivers[...], owned)
+    receiver_hot = jnp.concatenate(receiver_blocks, axis=1)
+    node_blocks = owned // 128
+    sender_hot = jnp.concatenate(sender_blocks[:node_blocks], axis=1)
+    ghost_hot = jnp.concatenate(sender_blocks[node_blocks:], axis=1)
+    own_lat = node_lat[...]
+    edge_in0 = edge_lat[...]
+    edge_in1 = narrow(matmul(sender_hot, own_lat) + matmul(ghost_hot, ghost_lat[...]))
+    edge_in2 = narrow(matmul(receiver_hot, own_lat))
+
+    pre = (
+        matmul(edge_in0, ew1[0:latent])
+        + matmul(edge_in1, ew1[latent : 2 * latent])
+        + matmul(edge_in2, ew1[2 * latent : 3 * latent])
+    )
+    e_act1, e_slope1 = activate(pre)
+    e_act2, e_slope2 = activate(matmul(e_act1, ew2[...]))
+    e_normed, e_norm = norm_parts(matmul(e_act2, ew3[...]))
+    updated = narrow(wide(edge_in0) + e_normed * egain[...])
+    summed = narrow(matmul(receiver_rows, updated))
+
+    pre = matmul(own_lat, nw1[0:latent]) + matmul(summed, nw1[latent : 2 * latent])
+    n_act1, n_slope1 = activate(pre)
+    n_act2, n_slope2 = activate(matmul(n_act1, nw2[...]))
+    n_normed, n_norm = norm_parts(matmul(n_act2, nw3[...]))
+    node_up = wide(node_cot[...])
+    n_gsum = jnp.sum(node_up * n_normed, axis=0, keepdims=True)
+    q3 = narrow(norm_back(node_up * ngain[...], n_normed, n_norm))
+    q2 = narrow(against(q3, nw3[...]) * n_slope2)
+    q1 = narrow(against(q2, nw2[...]) * n_slope1)
+    back_summed = narrow(against(q1, nw1[latent : 2 * latent]))
+    put(
+        0,
+        (
+            jnp.concatenate([over_rows(own_lat, q1), over_rows(summed, q1)], axis=0),
+            over_rows(n_act1, q2),
+            over_rows(n_act2, q3),
+        ),
+    )
+    pl.semaphore_wait(barrier, domains + 1)
+    over_core(0).start()
+
+    node_part = node_up + against(q1, nw1[0:latent])
+    edge_up = wide(edge_cot[...]) + matmul(receiver_hot, back_summed)
+    e_gsum = jnp.sum(edge_up * e_normed, axis=0, keepdims=True)
+    q3 = narrow(norm_back(edge_up * egain[...], e_normed, e_norm))
+    stage_pair(0)
+    q2 = narrow(against(q3, ew3[...]) * e_slope2)
+    row = lax.broadcasted_iota(jnp.int32, (16, half), 0)
+    tail = jnp.where(row == 0, e_gsum[:, :half], 0.0)
+    tail = jnp.where(row == 1, e_gsum[:, half:], tail)
+    tail = jnp.where(row == 2, n_gsum[:, :half], tail)
+    tail = narrow(jnp.where(row == 3, n_gsum[:, half:], tail))
+    put(1, (over_rows(e_act1, q2), over_rows(e_act2, q3)), tail)
+    over_core(1).start()
+    q1 = narrow(against(q2, ew2[...]) * e_slope1)
+    put(
+        2,
+        (
+            jnp.concatenate(
+                [over_rows(edge_in0, q1), over_rows(edge_in1, q1), over_rows(edge_in2, q1)],
+                axis=0,
+            ),
+        ),
+    )
+    over_core(2).start()
+    stage_pair(1)
+    stage_dom(0)
+
+    to_sender = narrow(against(q1, ew1[latent : 2 * latent]))
+    to_table = matmul(sender_rows, to_sender)
+    slot = lax.broadcasted_iota(jnp.int32, (slots, latent), 0)
+    halos = []
+    for direction, offset in enumerate(OFFSETS):
+        first = owned + direction * slots
+        live = slot < counts[:, direction : direction + 1]
+        ghost_out[direction] = narrow(jnp.where(live, to_table[first : first + slots], 0.0))
+        halo = remote(
+            ghost_out.at[direction],
+            ghost_in.at[direction],
+            3 * per_chunk + direction,
+            {"dom": ahead(offset)},
+        )
+        halo.start()
+        halos.append(halo)
+    stage_pair(2)
+    stage_dom(1)
+    to_receiver = narrow(against(q1, ew1[2 * latent : 3 * latent]))
+    node_part = node_part + to_table[:owned] + matmul(receiver_rows, to_receiver)
+    stage_spread(0)
+    grad_edge[...] = narrow(edge_up + against(q1, ew1[0:latent]))
+    stage_dom(2)
+    gains = stage_spread(1)
+    gains = gains[gains.shape[0] - 16 :]
+    quarter = latent // 4
+    for out, first, scale in ((out_eg, 0, edge_scale), (out_ng, 2, node_scale)):
+        line = jnp.where(pair == 0, gains[first : first + 1], gains[first + 1 : first + 2])
+        out[...] = jnp.where(core == 0, line[:, :quarter], line[:, quarter:]) * scale
+    for halo in halos:
+        halo.wait()
+    owner = lax.broadcasted_iota(jnp.int32, (owned, slots), 0)
+    for direction in range(4):
+        hot = one_hot(owner == recv_index[direction : direction + 1, :])
+        node_part = node_part + matmul(hot, ghost_in[direction])
+    grad_node[...] = narrow(node_part)
+    stage_out(0, (out_n1, out_n2, out_n3), node_scale)
+    stage_spread(2)
+    stage_out(1, (out_e2, out_e3), edge_scale)
+    stage_out(2, (out_e1,), edge_scale)
+
+
+def fused_device(
+    node_latents,
+    ghost_latents,
+    edge_latents,
+    node_cotangent,
+    edge_cotangent,
+    senders,
+    receivers,
+    halo_counts,
+    recv_index,
+    edge_w1,
+    edge_w2,
+    edge_w3,
+    edge_gain,
+    node_w1,
+    node_w2,
+    node_w3,
+    node_gain,
+):
+    domains = lax.axis_size("dom")
+    groups = lax.axis_size("grp")
+    nodes, latent = node_latents.shape[1:]
+    edges = edge_latents.shape[1]
+    slots = ghost_latents.shape[1] // 4
+    partitions = domains * groups
+    plan = (
+        domains,
+        1.0 / math.sqrt(partitions * edges),
+        1.0 / math.sqrt(partitions * nodes),
+    )
+    half = latent // 2
+    quarter = latent // 4
+    blocks = domains // 2
+    bulk = [
+        node_w1.shape[0] // 4 + 2 * quarter,
+        2 * quarter,
+        edge_w1.shape[0] // 4,
+    ]
+    clean = [rows // blocks for rows in bulk]
+    sizes = [clean[0], clean[1] + 16, clean[2]]
+
+    def buffers(lead, kind, rows=sizes):
+        return [pltpu.VMEM((*lead, size, half), kind) for size in rows]
+
+    scratch = (
+        buffers((2, 2, domains), jnp.bfloat16)
+        + buffers((2, domains), jnp.bfloat16)
+        + buffers((domains,), jnp.bfloat16)
+        + buffers((domains,), jnp.float32)
+        + buffers((domains,), jnp.bfloat16)
+        + buffers((domains,), jnp.bfloat16)
+        + buffers((domains,), jnp.bfloat16)
+        + buffers((domains,), jnp.bfloat16, clean)
+        + [
+            pltpu.VMEM((4, slots, latent), jnp.bfloat16),
+            pltpu.VMEM((4, slots, latent), jnp.bfloat16),
+        ]
+    )
+    copies = 3 * (2 + 2 * (domains - 1)) + 4
+    scratch += [pltpu.SemaphoreType.DMA((copies,)), pltpu.SemaphoreType.DMA((copies,))]
+    vmem = pl.BlockSpec(memory_space=pltpu.VMEM)
+
+    def grad(rows):
+        return jax.ShapeDtypeStruct((rows, latent), jnp.float32)
+
+    gain = jax.ShapeDtypeStruct((1, quarter), jnp.float32)
+    outs = pl.pallas_call(
+        functools.partial(fused_kernel, plan),
+        out_shape=(
+            jax.ShapeDtypeStruct((nodes, latent), jnp.bfloat16),
+            jax.ShapeDtypeStruct((edges, latent), jnp.bfloat16),
+            grad(edge_w1.shape[0] // 4),
+            grad(quarter),
+            grad(quarter),
+            gain,
+            grad(node_w1.shape[0] // 4),
+            grad(quarter),
+            grad(quarter),
+            gain,
+        ),
+        in_specs=[vmem] * 17,
+        out_specs=[vmem] * 10,
+        scratch_shapes=scratch,
+        compiler_params=pltpu.CompilerParams(
+            collective_id=0, has_side_effects=True, vmem_limit_bytes=48 * 1024 * 1024
+        ),
+    )(
+        node_latents[0],
+        ghost_latents[0],
+        edge_latents[0],
+        node_cotangent[0],
+        edge_cotangent[0],
+        senders,
+        receivers,
+        halo_counts,
+        recv_index[0],
+        edge_w1,
+        edge_w2,
+        edge_w3,
+        edge_gain[None],
+        node_w1,
+        node_w2,
+        node_w3,
+        node_gain[None],
+    )
+    outs = list(outs)
+    outs[0] = outs[0][None]
+    outs[1] = outs[1][None]
+    outs[5] = outs[5][0]
+    outs[9] = outs[9][0]
+    return tuple(outs)
+
+
 def solution(mesh):
     placed = (
         P("grp", "dom", None),
@@ -247,8 +702,10 @@
         P(),
         P(),
     )
+    domains, groups = mesh.shape["dom"], mesh.shape["grp"]
+    fits = groups == 4 and domains == 8
     return jax.shard_map(
-        per_device,
+        fused_device if fits else per_device,
         mesh=mesh,
         in_specs=placed,
         out_specs=(

time: 211 us -> 50.1 us (0.24)
  waiting for transfers between devices: 93.8 us -> 0 us
  blocking collectives: 49.5 us -> 0 us
  Pallas kernels: 0 us -> 31.9 us
  matrix products: 19.3 us -> 0 us
  between operations: 15.3 us -> 0.72 us
  starting transfers between devices: 13.4 us -> 0 us
  other arithmetic: 7.22 us -> 0 us
  local copies, waits for them, and re-layouts: 11.7 us -> 16.9 us
    reduce_scatter x6 -> x0, waiting for transfers between devices: 93.7 us -> none  [the longest x1 23.4 us: per_device(): lax.psum_scatter(edge_first.astype(jnp.bfloat16), 'grp', scatter_dimensio...]
    psum x1 -> x0, blocking collectives: 43.6 us -> none  [per_device(): lax.psum((reduced[0], reduced[1], reduced[2], reduced[3], reduced[4], red...]
    pallas_call x0 -> x1, Pallas kernels: none -> 31.9 us  [fused_device(): pl.pallas_call(functools.partial(fused_kernel, plan), out_shape=(jax.Shap...]
    dot_general x25 -> x0, matrix products: 19.3 us -> none  [the longest x9 9.55 us: over_rows(): lax.dot_general(left, right, (((0,), (0,)), ((), ())), preferred_element_...]
    ppermute x4 -> x0, starting transfers between devices: 13.1 us -> none  [from_behind(): return lax.ppermute(block, axis, route)]
    unnamed x73 -> x44, local copies, waits for them, and re-layouts: 9.99 us -> 16.9 us
    unnamed x1 -> x0, blocking collectives: 5.91 us -> none
    mul x8 -> x0, other arithmetic: 4.92 us -> none  [the longest x1 0.69 us: per_device(): reduced[0] * edge_scale]
  transfers between devices with their start and end apart: 10 -> 0, of which waited for: 5 -> 0; matrix products, arithmetic and copies ran while one was open for 9% -> 0% of each run, Pallas kernels for 0% -> 0%
where the time goes in v1:
time: 50.1 us; the launch traced here: 49.6 us
  Pallas kernels  31.9 us (64%)
  local copies, waits for them, and re-layouts  16.9 us (34%)
  between operations  0.72 us (1%)
    pallas_call x1, Pallas kernels, fused_device(): pl.pallas_call(functools.partial(fused_kernel, plan), out_shape=(jax.Shap...  31.9 us
    unnamed x44, local copies, waits for them, and re-layouts  16.9 us

profile of v1, /device:TPU:0, one launch (start us, length us, event | category | flops | bytes accessed | tf_op | source)
XLA Modules:
  0.0 49.6 jit_solution(16211567855347823924)
XLA Ops:
  0.6 0.0 copy-start.15
  0.7 0.0 copy-start.13
  0.7 0.0 copy-start.12
  0.7 0.0 copy-start.11
  0.7 0.0 copy-start.14
  0.7 0.0 copy-start.16
  0.7 0.6 %copy-done.15 = f32[256]{0:T(256)S(1)} copy-done((f32[256]{0:T(256)S(1)}, f32[256]{0:T(256)}, u32[]{:S(2)}) %copy-start.15) | copy-done | bytes 1048
  1.3 0.0 copy-done.13
  1.3 0.0 copy-done.12
  1.4 0.0 copy-done.11
  1.4 0.0 copy-done.14
  1.4 0.0 copy-done.16
  1.4 0.0 copy-start
  1.4 1.0 %copy-done = bf16[768,256]{1,0:T(8,128)(2,1)S(1)} copy-done((bf16[768,256]{1,0:T(8,128)(2,1)S(1)}, bf16[768,256]{1,0:T(8,128)(2,1)}, u32[]{:S(2)}) %copy-start) | copy-done | bytes 393240
  2.4 0.0 copy-start.1
  2.4 0.9 %copy-done.1 = bf16[1,512,256]{2,1,0:T(8,128)(2,1)S(1)} copy-done((bf16[1,512,256]{2,1,0:T(8,128)(2,1)S(1)}, bf16[1,512,256]{2,1,0:T(8,128)(2,1)}, u32[]{:S(2)}) %copy-start.1) | copy-done | bytes 262168
  3.3 0.0 copy-start.2
  3.3 0.9 %copy-done.2 = bf16[1,512,256]{2,1,0:T(8,128)(2,1)S(1)} copy-done((bf16[1,512,256]{2,1,0:T(8,128)(2,1)S(1)}, bf16[1,512,256]{2,1,0:T(8,128)(2,1)}, u32[]{:S(2)}) %copy-start.2) | copy-done | bytes 262168
  4.3 0.0 copy-start.3
  4.3 0.9 %copy-done.3 = bf16[512,256]{1,0:T(8,128)(2,1)S(1)} copy-done((bf16[512,256]{1,0:T(8,128)(2,1)S(1)}, bf16[512,256]{1,0:T(8,128)(2,1)}, u32[]{:S(2)}) %copy-start.3) | copy-done | bytes 262168
  5.2 0.0 copy-start.4
  5.2 0.9 %copy-done.4 = bf16[1,256,256]{2,1,0:T(8,128)(2,1)S(1)} copy-done((bf16[1,256,256]{2,1,0:T(8,128)(2,1)S(1)}, bf16[1,256,256]{2,1,0:T(8,128)(2,1)}, u32[]{:S(2)}) %copy-start.4) | copy-done | bytes 131096
  6.1 0.0 copy-start.5
  6.2 0.9 %copy-done.5 = bf16[1,256,256]{2,1,0:T(8,128)(2,1)S(1)} copy-done((bf16[1,256,256]{2,1,0:T(8,128)(2,1)S(1)}, bf16[1,256,256]{2,1,0:T(8,128)(2,1)}, u32[]{:S(2)}) %copy-start.5) | copy-done | bytes 131096
  7.1 0.0 copy-start.6
  7.1 0.9 %copy-done.6 = bf16[256,256]{1,0:T(8,128)(2,1)S(1)} copy-done((bf16[256,256]{1,0:T(8,128)(2,1)S(1)}, bf16[256,256]{1,0:T(8,128)(2,1)}, u32[]{:S(2)}) %copy-start.6) | copy-done | bytes 131096
  8.0 0.0 copy-start.7
  8.0 0.9 %copy-done.7 = bf16[256,256]{1,0:T(8,128)(2,1)S(1)} copy-done((bf16[256,256]{1,0:T(8,128)(2,1)S(1)}, bf16[256,256]{1,0:T(8,128)(2,1)}, u32[]{:S(2)}) %copy-start.7) | copy-done | bytes 131096
  8.9 0.0 copy-start.8
  8.9 0.9 %copy-done.8 = bf16[256,256]{1,0:T(8,128)(2,1)S(1)} copy-done((bf16[256,256]{1,0:T(8,128)(2,1)S(1)}, bf16[256,256]{1,0:T(8,128)(2,1)}, u32[]{:S(2)}) %copy-start.8) | copy-done | bytes 131096
  9.8 0.0 copy-start.9
  9.8 0.9 %copy-done.9 = bf16[256,256]{1,0:T(8,128)(2,1)S(1)} copy-done((bf16[256,256]{1,0:T(8,128)(2,1)S(1)}, bf16[256,256]{1,0:T(8,128)(2,1)}, u32[]{:S(2)}) %copy-start.9) | copy-done | bytes 131096
  10.7 0.0 copy-start.10
  10.7 0.8 %copy-done.10 = bf16[1,64,256]{2,1,0:T(8,128)(2,1)S(1)} copy-done((bf16[1,64,256]{2,1,0:T(8,128)(2,1)S(1)}, bf16[1,64,256]{2,1,0:T(8,128)(2,1)}, u32[]{:S(2)}) %copy-start.10) | copy-done | bytes 32792
  11.4 31.9 %shard_map.240 = (bf16[256,256]{1,0:T(8,128)(2,1)S(1)}, bf16[512,256]{1,0:T(8,128)(2,1)S(1)}, f32[192,256]{1,0:T(8,128)S(1)}, f32[64,256]{1,0:T(8,128)S(1)}, f32...) custom-call(bf16[256,256]{1,0:T(8,128)(2,1)S(1)} %bitcast.15, ...), custom_call_target="tpu_custom_call" | custom-call | tf_op jit(solution)/shard_map/pallas_call | solution.py:638
  43.4 0.7 %copy.37 = bf16[1,256,256]{2,1,0:T(8,128)(2,1)} copy(bf16[1,256,256]{2,1,0:T(8,128)(2,1)S(1)} %bitcast.17) | data formatting | bytes 262144
  44.0 0.7 %copy.38 = bf16[1,512,256]{2,1,0:T(8,128)(2,1)} copy(bf16[1,512,256]{2,1,0:T(8,128)(2,1)S(1)} %bitcast.14) | data formatting | bytes 524288
  44.7 0.7 %copy.39 = f32[192,256]{1,0:T(8,128)} copy(f32[192,256]{1,0:T(8,128)S(1)} %get-tuple-element.42) | data formatting | bytes 393216
  45.4 0.6 %copy.40 = f32[64,256]{1,0:T(8,128)} copy(f32[64,256]{1,0:T(8,128)S(1)} %get-tuple-element.43) | data formatting | bytes 131072
  46.0 0.6 %copy.41 = f32[64,256]{1,0:T(8,128)} copy(f32[64,256]{1,0:T(8,128)S(1)} %get-tuple-element.44) | data formatting | bytes 131072
  46.7 0.5 %copy.42 = f32[64]{0:T(128)} copy(f32[64]{0:T(128)S(1)} %bitcast.23) | data formatting | bytes 512
  47.2 0.7 %copy.43 = f32[128,256]{1,0:T(8,128)} copy(f32[128,256]{1,0:T(8,128)S(1)} %get-tuple-element.46) | data formatting | bytes 262144
  47.8 0.6 %copy.44 = f32[64,256]{1,0:T(8,128)} copy(f32[64,256]{1,0:T(8,128)S(1)} %get-tuple-element.47) | data formatting | bytes 131072
  48.5 0.6 %copy.45 = f32[64,256]{1,0:T(8,128)} copy(f32[64,256]{1,0:T(8,128)S(1)} %get-tuple-element.48) | data formatting | bytes 131072
  49.1 0.5 %copy.46 = f32[64]{0:T(128)} copy(f32[64]{0:T(128)S(1)} %bitcast.22) | data formatting | bytes 512
Async XLA Ops:
  0.6 0.7 %copy-start.15 = (f32[256]{0:T(256)S(1)}, f32[256]{0:T(256)}, u32[]{:S(2)}) copy-start(f32[256]{0:T(256)} %param.33) | copy-start | bytes 3076
  0.7 0.7 %copy-start.13 = (s32[1,4,16]{2,1,0:T(4,128)S(1)}, s32[1,4,16]{2,1,0:T(4,128)}, u32[]{:S(2)}) copy-start(s32[1,4,16]{2,1,0:T(4,128)} %param.25) | copy-start | bytes 772
  0.7 0.7 %copy-start.12 = (s32[1,512]{1,0:T(1,128)S(1)}, s32[1,512]{1,0:T(1,128)}, u32[]{:S(2)}) copy-start(s32[1,512]{1,0:T(1,128)} %receivers.1) | copy-start | bytes 6148
  0.7 0.7 %copy-start.11 = (s32[1,512]{1,0:T(1,128)S(1)}, s32[1,512]{1,0:T(1,128)}, u32[]{:S(2)}) copy-start(s32[1,512]{1,0:T(1,128)} %senders.1) | copy-start | bytes 6148
  0.7 0.7 %copy-start.14 = (f32[256]{0:T(256)S(1)}, f32[256]{0:T(256)}, u32[]{:S(2)}) copy-start(f32[256]{0:T(256)} %param.29) | copy-start | bytes 3076
  0.7 0.7 %copy-start.16 = (s32[1,4]{1,0:T(1,128)S(1)}, s32[1,4]{1,0:T(1,128)}, u32[]{:S(2)}) copy-start(s32[1,4]{1,0:T(1,128)} %counts.1) | copy-start | bytes 52
  1.4 1.0 %copy-start = (bf16[768,256]{1,0:T(8,128)(2,1)S(1)}, bf16[768,256]{1,0:T(8,128)(2,1)}, u32[]{:S(2)}) copy-start(bf16[768,256]{1,0:T(8,128)(2,1)} %ew1.1) | copy-start | bytes 1179652
  2.4 0.9 %copy-start.1 = (bf16[1,512,256]{2,1,0:T(8,128)(2,1)S(1)}, bf16[1,512,256]{2,1,0:T(8,128)(2,1)}, u32[]{:S(2)}) copy-start(bf16[1,512,256]{2,1,0:T(8,128)(2,1)} %param.19) | copy-start | bytes 786436
  3.3 0.9 %copy-start.2 = (bf16[1,512,256]{2,1,0:T(8,128)(2,1)S(1)}, bf16[1,512,256]{2,1,0:T(8,128)(2,1)}, u32[]{:S(2)}) copy-start(bf16[1,512,256]{2,1,0:T(8,128)(2,1)} %param.21) | copy-start | bytes 786436
  4.3 0.9 %copy-start.3 = (bf16[512,256]{1,0:T(8,128)(2,1)S(1)}, bf16[512,256]{1,0:T(8,128)(2,1)}, u32[]{:S(2)}) copy-start(bf16[512,256]{1,0:T(8,128)(2,1)} %nw1.1) | copy-start | bytes 786436
  5.2 0.9 %copy-start.4 = (bf16[1,256,256]{2,1,0:T(8,128)(2,1)S(1)}, bf16[1,256,256]{2,1,0:T(8,128)(2,1)}, u32[]{:S(2)}) copy-start(bf16[1,256,256]{2,1,0:T(8,128)(2,1)} %param.17) | copy-start | bytes 393220
  6.1 0.9 %copy-start.5 = (bf16[1,256,256]{2,1,0:T(8,128)(2,1)S(1)}, bf16[1,256,256]{2,1,0:T(8,128)(2,1)}, u32[]{:S(2)}) copy-start(bf16[1,256,256]{2,1,0:T(8,128)(2,1)} %param.20) | copy-start | bytes 393220
  7.1 0.9 %copy-start.6 = (bf16[256,256]{1,0:T(8,128)(2,1)S(1)}, bf16[256,256]{1,0:T(8,128)(2,1)}, u32[]{:S(2)}) copy-start(bf16[256,256]{1,0:T(8,128)(2,1)} %ew2.1) | copy-start | bytes 393220
  8.0 0.9 %copy-start.7 = (bf16[256,256]{1,0:T(8,128)(2,1)S(1)}, bf16[256,256]{1,0:T(8,128)(2,1)}, u32[]{:S(2)}) copy-start(bf16[256,256]{1,0:T(8,128)(2,1)} %ew3.1) | copy-start | bytes 393220
  8.9 0.9 %copy-start.8 = (bf16[256,256]{1,0:T(8,128)(2,1)S(1)}, bf16[256,256]{1,0:T(8,128)(2,1)}, u32[]{:S(2)}) copy-start(bf16[256,256]{1,0:T(8,128)(2,1)} %nw2.1) | copy-start | bytes 393220
  9.8 0.9 %copy-start.9 = (bf16[256,256]{1,0:T(8,128)(2,1)S(1)}, bf16[256,256]{1,0:T(8,128)(2,1)}, u32[]{:S(2)}) copy-start(bf16[256,256]{1,0:T(8,128)(2,1)} %nw3.1) | copy-start | bytes 393220
  10.7 0.8 %copy-start.10 = (bf16[1,64,256]{2,1,0:T(8,128)(2,1)S(1)}, bf16[1,64,256]{2,1,0:T(8,128)(2,1)}, u32[]{:S(2)}) copy-start(bf16[1,64,256]{2,1,0:T(8,128)(2,1)} %param.18) | copy-start | bytes 98308

commit v2 on v1

--- a/solution.py
+++ b/solution.py
@@ -264,23 +264,23 @@
 
 def fused_kernel(
     plan,
-    node_lat,
-    ghost_lat,
-    edge_lat,
-    node_cot,
-    edge_cot,
-    senders,
-    receivers,
-    counts,
-    recv_index,
-    ew1,
-    ew2,
-    ew3,
-    egain,
-    nw1,
-    nw2,
-    nw3,
-    ngain,
+    node_lat_hbm,
+    ghost_lat_hbm,
+    edge_lat_hbm,
+    node_cot_hbm,
+    edge_cot_hbm,
+    senders_hbm,
+    receivers_hbm,
+    counts_hbm,
+    recv_index_hbm,
+    ew1_hbm,
+    ew2_hbm,
+    ew3_hbm,
+    egain_hbm,
+    nw1_hbm,
+    nw2_hbm,
+    nw3_hbm,
+    ngain_hbm,
     grad_node,
     grad_edge,
     out_e1,
@@ -319,7 +319,53 @@
     ghost_in,
     send_sem,
     recv_sem,
+    load_sem,
+    node_lat,
+    ghost_lat,
+    edge_lat,
+    node_cot,
+    edge_cot,
+    senders,
+    receivers,
+    counts,
+    recv_index,
+    ew1,
+    ew2,
+    ew3,
+    egain,
+    nw1,
+    nw2,
+    nw3,
+    ngain,
 ):
+    loads = {}
+    for source, staged in (
+        (senders_hbm, senders),
+        (receivers_hbm, receivers),
+        (node_lat_hbm, node_lat),
+        (ghost_lat_hbm, ghost_lat),
+        (edge_lat_hbm, edge_lat),
+        (ew1_hbm, ew1),
+        (ew2_hbm, ew2),
+        (ew3_hbm, ew3),
+        (egain_hbm, egain),
+        (nw1_hbm, nw1),
+        (nw2_hbm, nw2),
+        (nw3_hbm, nw3),
+        (node_cot_hbm, node_cot),
+        (ngain_hbm, ngain),
+        (edge_cot_hbm, edge_cot),
+        (counts_hbm, counts),
+        (recv_index_hbm, recv_index),
+    ):
+        load = pltpu.make_async_copy(source, staged, load_sem.at[len(loads)])
+        load.start()
+        loads[len(loads)] = load
+
+    def need(first, last):
+        for number in range(first, last):
+            loads[number].wait()
+
     domains, edge_scale, node_scale = plan
     latent = node_lat.shape[1]
     owned = node_lat.shape[0]
@@ -457,17 +503,20 @@
                     ]
                 base += out.shape[0]
 
+    need(0, 2)
     sender_blocks, sender_rows = hot_pair(senders[...], owned + ghosts)
     receiver_blocks, receiver_rows = hot_pair(receivers[...], owned)
     receiver_hot = jnp.concatenate(receiver_blocks, axis=1)
     node_blocks = owned // 128
     sender_hot = jnp.concatenate(sender_blocks[:node_blocks], axis=1)
     ghost_hot = jnp.concatenate(sender_blocks[node_blocks:], axis=1)
+    need(2, 5)
     own_lat = node_lat[...]
     edge_in0 = edge_lat[...]
     edge_in1 = narrow(matmul(sender_hot, own_lat) + matmul(ghost_hot, ghost_lat[...]))
     edge_in2 = narrow(matmul(receiver_hot, own_lat))
 
+    need(5, 9)
     pre = (
         matmul(edge_in0, ew1[0:latent])
         + matmul(edge_in1, ew1[latent : 2 * latent])
@@ -479,6 +528,7 @@
     updated = narrow(wide(edge_in0) + e_normed * egain[...])
     summed = narrow(matmul(receiver_rows, updated))
 
+    need(9, 17)
     pre = matmul(own_lat, nw1[0:latent]) + matmul(summed, nw1[latent : 2 * latent])
     n_act1, n_slope1 = activate(pre)
     n_act2, n_slope2 = activate(matmul(n_act1, nw2[...]))
@@ -569,6 +619,16 @@
     stage_out(2, (out_e1,), edge_scale)
 
 
+def store_kernel(*refs):
+    copies = [
+        pltpu.make_async_copy(refs[at], refs[at + 10], refs[20].at[at]) for at in range(10)
+    ]
+    for copy in copies:
+        copy.start()
+    for copy in copies:
+        copy.wait()
+
+
 def fused_device(
     node_latents,
     ghost_latents,
@@ -629,33 +689,7 @@
     )
     copies = 3 * (2 + 2 * (domains - 1)) + 4
     scratch += [pltpu.SemaphoreType.DMA((copies,)), pltpu.SemaphoreType.DMA((copies,))]
-    vmem = pl.BlockSpec(memory_space=pltpu.VMEM)
-
-    def grad(rows):
-        return jax.ShapeDtypeStruct((rows, latent), jnp.float32)
-
-    gain = jax.ShapeDtypeStruct((1, quarter), jnp.float32)
-    outs = pl.pallas_call(
-        functools.partial(fused_kernel, plan),
-        out_shape=(
-            jax.ShapeDtypeStruct((nodes, latent), jnp.bfloat16),
-            jax.ShapeDtypeStruct((edges, latent), jnp.bfloat16),
-            grad(edge_w1.shape[0] // 4),
-            grad(quarter),
-            grad(quarter),
-            gain,
-            grad(node_w1.shape[0] // 4),
-            grad(quarter),
-            grad(quarter),
-            gain,
-        ),
-        in_specs=[vmem] * 17,
-        out_specs=[vmem] * 10,
-        scratch_shapes=scratch,
-        compiler_params=pltpu.CompilerParams(
-            collective_id=0, has_side_effects=True, vmem_limit_bytes=48 * 1024 * 1024
-        ),
-    )(
+    operands = (
         node_latents[0],
         ghost_latents[0],
         edge_latents[0],
@@ -674,6 +708,43 @@
         node_w3,
         node_gain[None],
     )
+    scratch += [pltpu.SemaphoreType.DMA((len(operands),))]
+    scratch += [pltpu.VMEM(operand.shape, operand.dtype) for operand in operands]
+    vmem = pl.BlockSpec(memory_space=pltpu.VMEM)
+
+    def grad(rows):
+        return jax.ShapeDtypeStruct((rows, latent), jnp.float32)
+
+    gain = jax.ShapeDtypeStruct((1, quarter), jnp.float32)
+    outs = pl.pallas_call(
+        functools.partial(fused_kernel, plan),
+        out_shape=(
+            jax.ShapeDtypeStruct((nodes, latent), jnp.bfloat16),
+            jax.ShapeDtypeStruct((edges, latent), jnp.bfloat16),
+            grad(edge_w1.shape[0] // 4),
+            grad(quarter),
+            grad(quarter),
+            gain,
+            grad(node_w1.shape[0] // 4),
+            grad(quarter),
+            grad(quarter),
+            gain,
+        ),
+        in_specs=[pl.BlockSpec(memory_space=pltpu.HBM)] * len(operands),
+        out_specs=[vmem] * 10,
+        scratch_shapes=scratch,
+        compiler_params=pltpu.CompilerParams(
+            collective_id=0, has_side_effects=True, vmem_limit_bytes=60 * 1024 * 1024
+        ),
+    )(*operands)
+    outs = pl.pallas_call(
+        store_kernel,
+        out_shape=tuple(jax.ShapeDtypeStruct(out.shape, out.dtype) for out in outs),
+        in_specs=[pl.BlockSpec(memory_space=pltpu.HBM)] * 10,
+        out_specs=[pl.BlockSpec(memory_space=pltpu.HBM)] * 10,
+        scratch_shapes=[pltpu.SemaphoreType.DMA((10,))],
+        compiler_params=pltpu.CompilerParams(vmem_limit_bytes=60 * 1024 * 1024),
+    )(*outs)
     outs = list(outs)
     outs[0] = outs[0][None]
     outs[1] = outs[1][None]

time: 50.1 us -> 65 us (1.30)
  Pallas kernels: 31.9 us -> 64.2 us
  local copies, waits for them, and re-layouts: 16.9 us -> 0 us
    pallas_call x0 -> x1, Pallas kernels: none -> 31 us  [fused_device(): pl.pallas_call(store_kernel, out_shape=tuple((jax.ShapeDtypeStruct(out.sh...]
    unnamed x44 -> x0, local copies, waits for them, and re-layouts: 16.9 us -> none
    pallas_call x1, Pallas kernels: 31.9 us -> 33.1 us  [fused_device(): pl.pallas_call(functools.partial(fused_kernel, plan), out_shape=(jax.Shap...]
where the time goes in v2:
time: 65 us; the launch traced here: 64.8 us
  Pallas kernels  64.2 us (99%)
  between operations  0.66 us (1%)
    pallas_call x1, Pallas kernels, fused_device(): pl.pallas_call(functools.partial(fused_kernel, plan), out_shape=(jax.Shap...  33.1 us
    pallas_call x1, Pallas kernels, fused_device(): pl.pallas_call(store_kernel, out_shape=tuple((jax.ShapeDtypeStruct(out.sh...  31 us

profile of v2, /device:TPU:0, one launch (start us, length us, event | category | flops | bytes accessed | tf_op | source)
XLA Modules:
  0.0 64.8 jit_solution(16472964179044436313)
XLA Ops:
  0.6 33.1 %shard_map.240 = (bf16[256,256]{1,0:T(8,128)(2,1)}, bf16[512,256]{1,0:T(8,128)(2,1)}, f32[192,256]{1,0:T(8,128)}, f32[64,256]{1,0:T(8,128)}, f32[64,256]{1,0:T(8...) custom-call(bf16[256,256]{1,0:T(8,128)(2,1)} %bitcast.14, ...), custom_call_target="tpu_custom_call" | custom-call | tf_op jit(solution)/shard_map/pallas_call | solution.py:719
  33.8 31.0 %shard_map.241 = (bf16[256,256]{1,0:T(8,128)(2,1)}, bf16[512,256]{1,0:T(8,128)(2,1)}, f32[192,256]{1,0:T(8,128)}, f32[64,256]{1,0:T(8,128)}, f32[64,256]{1,0:T(8...) custom-call(bf16[256,256]{1,0:T(8,128)(2,1)} %get-tuple-element.30.r, ...), custom_call_target="tpu_custom_call" | custom-call | tf_op jit(solution)/shard_map/pallas_call | solution.py:740

commit v3 on v2

--- a/solution.py
+++ b/solution.py
@@ -564,6 +564,7 @@
     put(1, (over_rows(e_act1, q2), over_rows(e_act2, q3)), tail)
     over_core(1).start()
     q1 = narrow(against(q2, ew2[...]) * e_slope1)
+    stage_dom(0)
     put(
         2,
         (
@@ -575,7 +576,6 @@
     )
     over_core(2).start()
     stage_pair(1)
-    stage_dom(0)
 
     to_sender = narrow(against(q1, ew1[latent : 2 * latent]))
     to_table = matmul(sender_rows, to_sender)
@@ -620,13 +620,17 @@
 
 
 def store_kernel(*refs):
-    copies = [
-        pltpu.make_async_copy(refs[at], refs[at + 10], refs[20].at[at]) for at in range(10)
-    ]
-    for copy in copies:
-        copy.start()
-    for copy in copies:
-        copy.wait()
+    ins, outs, held = refs[:10], refs[10:20], refs[20:30]
+    load_sem, store_sem = refs[30:]
+    loads = [pltpu.make_async_copy(ins[at], held[at], load_sem.at[at]) for at in range(10)]
+    stores = [pltpu.make_async_copy(held[at], outs[at], store_sem.at[at]) for at in range(10)]
+    for load in loads:
+        load.start()
+    for load, store in zip(loads, stores):
+        load.wait()
+        store.start()
+    for store in stores:
+        store.wait()
 
 
 def fused_device(
@@ -742,7 +746,8 @@
         out_shape=tuple(jax.ShapeDtypeStruct(out.shape, out.dtype) for out in outs),
         in_specs=[pl.BlockSpec(memory_space=pltpu.HBM)] * 10,
         out_specs=[pl.BlockSpec(memory_space=pltpu.HBM)] * 10,
-        scratch_shapes=[pltpu.SemaphoreType.DMA((10,))],
+        scratch_shapes=[pltpu.VMEM(out.shape, out.dtype) for out in outs]
+        + [pltpu.SemaphoreType.DMA((10,)), pltpu.SemaphoreType.DMA((10,))],
         compiler_params=pltpu.CompilerParams(vmem_limit_bytes=60 * 1024 * 1024),
     )(*outs)
     outs = list(outs)

time: 65 us -> 36.6 us (0.56)
  Pallas kernels: 64.2 us -> 35.8 us
    pallas_call x1, Pallas kernels: 31 us -> 2.1 us  [fused_device(): pl.pallas_call(store_kernel, out_shape=tuple((jax.ShapeDtypeStruct(out.sh...]
where the time goes in v3:
time: 36.6 us; the launch traced here: 36.5 us
  Pallas kernels  35.8 us (98%)
  between operations  0.66 us (2%)
    pallas_call x1, Pallas kernels, fused_device(): pl.pallas_call(functools.partial(fused_kernel, plan), out_shape=(jax.Shap...  33.7 us
    pallas_call x1, Pallas kernels, fused_device(): pl.pallas_call(store_kernel, out_shape=tuple((jax.ShapeDtypeStruct(out.sh...  2.1 us

profile of v3, /device:TPU:0, one launch (start us, length us, event | category | flops | bytes accessed | tf_op | source)
XLA Modules:
  0.0 36.5 jit_solution(2862936154420060750)
XLA Ops:
  0.6 33.7 %shard_map.240 = (bf16[256,256]{1,0:T(8,128)(2,1)}, bf16[512,256]{1,0:T(8,128)(2,1)}, f32[192,256]{1,0:T(8,128)}, f32[64,256]{1,0:T(8,128)}, f32[64,256]{1,0:T(8...) custom-call(bf16[256,256]{1,0:T(8,128)(2,1)} %bitcast.14, ...), custom_call_target="tpu_custom_call" | custom-call | tf_op jit(solution)/shard_map/pallas_call | solution.py:723
  34.4 2.1 %shard_map.241 = (bf16[256,256]{1,0:T(8,128)(2,1)}, bf16[512,256]{1,0:T(8,128)(2,1)}, f32[192,256]{1,0:T(8,128)}, f32[64,256]{1,0:T(8,128)}, f32[64,256]{1,0:T(8...) custom-call(bf16[256,256]{1,0:T(8,128)(2,1)} %get-tuple-element.30.r, ...), custom_call_target="tpu_custom_call" | custom-call | tf_op jit(solution)/shard_map/pallas_call | solution.py:744

commit v4 on v3

--- a/solution.py
+++ b/solution.py
@@ -281,16 +281,16 @@
     nw2_hbm,
     nw3_hbm,
     ngain_hbm,
-    grad_node,
-    grad_edge,
-    out_e1,
-    out_e2,
-    out_e3,
-    out_eg,
-    out_n1,
-    out_n2,
-    out_n3,
-    out_ng,
+    grad_node_hbm,
+    grad_edge_hbm,
+    out_e1_hbm,
+    out_e2_hbm,
+    out_e3_hbm,
+    out_eg_hbm,
+    out_n1_hbm,
+    out_n2_hbm,
+    out_n3_hbm,
+    out_ng_hbm,
     terms_n,
     terms_b,
     terms_c,
@@ -337,7 +337,35 @@
     nw2,
     nw3,
     ngain,
+    save_sem,
+    grad_node,
+    grad_edge,
+    out_e1,
+    out_e2,
+    out_e3,
+    out_eg,
+    out_n1,
+    out_n2,
+    out_n3,
+    out_ng,
 ):
+    saves = [
+        pltpu.make_async_copy(staged, target, save_sem.at[number])
+        for number, (staged, target) in enumerate(
+            (
+                (grad_node, grad_node_hbm),
+                (grad_edge, grad_edge_hbm),
+                (out_e1, out_e1_hbm),
+                (out_e2, out_e2_hbm),
+                (out_e3, out_e3_hbm),
+                (out_eg, out_eg_hbm),
+                (out_n1, out_n1_hbm),
+                (out_n2, out_n2_hbm),
+                (out_n3, out_n3_hbm),
+                (out_ng, out_ng_hbm),
+            )
+        )
+    ]
     loads = {}
     for source, staged in (
         (senders_hbm, senders),
@@ -598,8 +626,9 @@
     to_receiver = narrow(against(q1, ew1[2 * latent : 3 * latent]))
     node_part = node_part + to_table[:owned] + matmul(receiver_rows, to_receiver)
     stage_spread(0)
+    stage_dom(2)
     grad_edge[...] = narrow(edge_up + against(q1, ew1[0:latent]))
-    stage_dom(2)
+    saves[1].start()
     gains = stage_spread(1)
     gains = gains[gains.shape[0] - 16 :]
     quarter = latent // 4
@@ -613,10 +642,19 @@
         hot = one_hot(owner == recv_index[direction : direction + 1, :])
         node_part = node_part + matmul(hot, ghost_in[direction])
     grad_node[...] = narrow(node_part)
+    for number in (0, 5, 9):
+        saves[number].start()
+    stage_spread(2)
     stage_out(0, (out_n1, out_n2, out_n3), node_scale)
-    stage_spread(2)
+    for number in (6, 7, 8):
+        saves[number].start()
     stage_out(1, (out_e2, out_e3), edge_scale)
+    for number in (3, 4):
+        saves[number].start()
     stage_out(2, (out_e1,), edge_scale)
+    saves[2].start()
+    for save in saves:
+        save.wait()
 
 
 def store_kernel(*refs):
@@ -714,28 +752,30 @@
     )
     scratch += [pltpu.SemaphoreType.DMA((len(operands),))]
     scratch += [pltpu.VMEM(operand.shape, operand.dtype) for operand in operands]
-    vmem = pl.BlockSpec(memory_space=pltpu.VMEM)
 
     def grad(rows):
         return jax.ShapeDtypeStruct((rows, latent), jnp.float32)
 
     gain = jax.ShapeDtypeStruct((1, quarter), jnp.float32)
+    shapes = (
+        jax.ShapeDtypeStruct((nodes, latent), jnp.bfloat16),
+        jax.ShapeDtypeStruct((edges, latent), jnp.bfloat16),
+        grad(edge_w1.shape[0] // 4),
+        grad(quarter),
+        grad(quarter),
+        gain,
+        grad(node_w1.shape[0] // 4),
+        grad(quarter),
+        grad(quarter),
+        gain,
+    )
+    scratch += [pltpu.SemaphoreType.DMA((len(shapes),))]
+    scratch += [pltpu.VMEM(out.shape, out.dtype) for out in shapes]
     outs = pl.pallas_call(
         functools.partial(fused_kernel, plan),
-        out_shape=(
-            jax.ShapeDtypeStruct((nodes, latent), jnp.bfloat16),
-            jax.ShapeDtypeStruct((edges, latent), jnp.bfloat16),
-            grad(edge_w1.shape[0] // 4),
-            grad(quarter),
-            grad(quarter),
-            gain,
-            grad(node_w1.shape[0] // 4),
-            grad(quarter),
-            grad(quarter),
-            gain,
-        ),
+        out_shape=shapes,
         in_specs=[pl.BlockSpec(memory_space=pltpu.HBM)] * len(operands),
-        out_specs=[vmem] * 10,
+        out_specs=[pl.BlockSpec(memory_space=pltpu.HBM)] * 10,
         scratch_shapes=scratch,
         compiler_params=pltpu.CompilerParams(
             collective_id=0, has_side_effects=True, vmem_limit_bytes=60 * 1024 * 1024

time: 36.6 us -> 36.4 us (level)
  no operation moved by 1% of the time
where the time goes in v4:
time: 36.4 us; the launch traced here: 36.3 us
  Pallas kernels  35.6 us (98%)
  between operations  0.66 us (2%)
    pallas_call x1, Pallas kernels, fused_device(): pl.pallas_call(functools.partial(fused_kernel, plan), out_shape=shapes, i...  33.5 us
    pallas_call x1, Pallas kernels, fused_device(): pl.pallas_call(store_kernel, out_shape=tuple((jax.ShapeDtypeStruct(out.sh...  2.1 us

profile of v4, /device:TPU:0, one launch (start us, length us, event | category | flops | bytes accessed | tf_op | source)
XLA Modules:
  0.0 36.3 jit_solution(6025893431646938985)
XLA Ops:
  0.6 33.5 %shard_map.240 = (bf16[256,256]{1,0:T(8,128)(2,1)}, bf16[512,256]{1,0:T(8,128)(2,1)}, f32[192,256]{1,0:T(8,128)}, f32[64,256]{1,0:T(8,128)}, f32[64,256]{1,0:T(8...) custom-call(bf16[256,256]{1,0:T(8,128)(2,1)} %bitcast.14, ...), custom_call_target="tpu_custom_call" | custom-call | tf_op jit(solution)/shard_map/pallas_call | solution.py:774
  34.2 2.1 %shard_map.241 = (bf16[256,256]{1,0:T(8,128)(2,1)}, bf16[512,256]{1,0:T(8,128)(2,1)}, f32[192,256]{1,0:T(8,128)}, f32[64,256]{1,0:T(8,128)}, f32[64,256]{1,0:T(8...) custom-call(bf16[256,256]{1,0:T(8,128)(2,1)} %get-tuple-element.30.r, ...), custom_call_target="tpu_custom_call" | custom-call | tf_op jit(solution)/shard_map/pallas_call | solution.py:784

commit v5 on v4

--- a/solution.py
+++ b/solution.py
@@ -475,8 +475,35 @@
             for step in range(1, domains)
         ]
 
+    column = lax.rem(dom, 2)
+    line = lax.div(dom, 2)
+
+    def across(number):
+        fin = chunks[number][7]
+        return remote(
+            fin.at[pl.ds(0, blocks)],
+            fin.at[pl.ds(blocks, blocks)],
+            number * per_chunk + domains + blocks,
+            {"dom": dom + 1 - 2 * column},
+        )
+
+    def stage_across(number):
+        for copy in spread(number):
+            copy.wait()
+        across(number).start()
+
     def spread(number):
         fin = chunks[number][7]
+        if number < 2:
+            return [
+                remote(
+                    fin.at[0],
+                    fin.at[step],
+                    number * per_chunk + domains + step,
+                    {"dom": ahead(2 * step)},
+                )
+                for step in range(1, blocks)
+            ]
         return [
             remote(
                 fin.at[0],
@@ -515,11 +542,15 @@
 
     def stage_out(number, outs, scale):
         fin = chunks[number][7]
-        for copy in spread(number):
+        for copy in [across(number)] if number < 2 else spread(number):
             copy.wait()
         size = fin.shape[1]
         for piece in range(domains):
-            value = wide(fin[lax.rem(dom - piece + domains, domains)]) * scale
+            slot = lax.rem(dom - piece + domains, domains)
+            if number < 2:
+                turn = lax.rem(column + piece, 2)
+                slot = turn * blocks + lax.rem(line - piece // 2 + blocks, blocks)
+            value = wide(fin[slot]) * scale
             lane = (piece % 2) * half
             first = (piece // 2) * size
             base = 0
@@ -633,18 +664,20 @@
     gains = gains[gains.shape[0] - 16 :]
     quarter = latent // 4
     for out, first, scale in ((out_eg, 0, edge_scale), (out_ng, 2, node_scale)):
-        line = jnp.where(pair == 0, gains[first : first + 1], gains[first + 1 : first + 2])
-        out[...] = jnp.where(core == 0, line[:, :quarter], line[:, quarter:]) * scale
+        gain_line = jnp.where(pair == 0, gains[first : first + 1], gains[first + 1 : first + 2])
+        out[...] = jnp.where(core == 0, gain_line[:, :quarter], gain_line[:, quarter:]) * scale
     for halo in halos:
         halo.wait()
     owner = lax.broadcasted_iota(jnp.int32, (owned, slots), 0)
     for direction in range(4):
         hot = one_hot(owner == recv_index[direction : direction + 1, :])
         node_part = node_part + matmul(hot, ghost_in[direction])
+    stage_across(0)
     grad_node[...] = narrow(node_part)
     for number in (0, 5, 9):
         saves[number].start()
     stage_spread(2)
+    stage_across(1)
     stage_out(0, (out_n1, out_n2, out_n3), node_scale)
     for number in (6, 7, 8):
         saves[number].start()

time: 36.4 us -> 34.5 us (0.948)
  Pallas kernels: 35.6 us -> 33.7 us
    pallas_call x1, Pallas kernels: 33.5 us -> 31.6 us  [fused_device(): pl.pallas_call(functools.partial(fused_kernel, plan), out_shape=shapes, i...]
where the time goes in v5:
time: 34.5 us; the launch traced here: 34.4 us
  Pallas kernels  33.7 us (98%)
  between operations  0.66 us (2%)
    pallas_call x1, Pallas kernels, fused_device(): pl.pallas_call(functools.partial(fused_kernel, plan), out_shape=shapes, i...  31.6 us
    pallas_call x1, Pallas kernels, fused_device(): pl.pallas_call(store_kernel, out_shape=tuple((jax.ShapeDtypeStruct(out.sh...  2.1 us

profile of v5, /device:TPU:0, one launch (start us, length us, event | category | flops | bytes accessed | tf_op | source)
XLA Modules:
  0.0 34.4 jit_solution(16229383024464266633)
XLA Ops:
  0.6 31.6 %shard_map.240 = (bf16[256,256]{1,0:T(8,128)(2,1)}, bf16[512,256]{1,0:T(8,128)(2,1)}, f32[192,256]{1,0:T(8,128)}, f32[64,256]{1,0:T(8,128)}, f32[64,256]{1,0:T(8...) custom-call(bf16[256,256]{1,0:T(8,128)(2,1)} %bitcast.14, ...), custom_call_target="tpu_custom_call" | custom-call | tf_op jit(solution)/shard_map/pallas_call | solution.py:807
  32.3 2.1 %shard_map.241 = (bf16[256,256]{1,0:T(8,128)(2,1)}, bf16[512,256]{1,0:T(8,128)(2,1)}, f32[192,256]{1,0:T(8,128)}, f32[64,256]{1,0:T(8,128)}, f32[64,256]{1,0:T(8...) custom-call(bf16[256,256]{1,0:T(8,128)(2,1)} %get-tuple-element.30.r, ...), custom_call_target="tpu_custom_call" | custom-call | tf_op jit(solution)/shard_map/pallas_call | solution.py:817
